TPU v7x, 32 devices: a whole 2x2x4 slice. The times are simulated.
32 devices in a mesh: dp: 8 (over y, x, core), tensor: 4 (over z).
Axes of the slice: x: 2, y: 2, z: 4, core: 2. Of those that a mesh axis runs over, the one named last changes fastest.
Arguments:
- x_tokens: bfloat16 [512, 8192], P('dp', 'tensor'), may hold values from -6 to 6
- sign_bits: int32 [8192], P('tensor'), may hold values from 0 to 1
- weight: bfloat16 [8192, 28672], P('tensor', 'dp'), may hold values from -0.0625 to 0.0625
- upstream: bfloat16 [512, 28672], P('tensor', 'dp'), may hold values from -0.25 to 0.25
Outputs:
- projected: bfloat16 [512, 28672], P('tensor', 'dp')
- weight_grad: float32 [8192, 28672], P('tensor', 'dp')
All inputs are finite; a program needn't handle non-finite values.
Results may differ from a plain program's by a relative error of at most 0.028.
Values may be sent and summed in bfloat16 or wider, within the bound.
No kernel may reach another device: no remote copies, remote signals or barrier semaphores. Data moves between devices by JAX's collectives and lax.ppermute only.
A program may use at most 128 MiB of HBM per device.

v0:
```python
import math

import jax
import jax.numpy as jnp
from jax import lax
from jax.sharding import PartitionSpec as P


def partner_2(block, axis, stride):
    count = lax.axis_size(axis)
    route = []
    for low in range(count):
        high = low | 1 << stride
        if high != low and high < count:
            route += [(low, high), (high, low)]
    return lax.ppermute(block, axis, route)


def hadamard(order):
    row_ids = jnp.arange(order, dtype=jnp.int32)[:, None]
    col_ids = jnp.arange(order, dtype=jnp.int32)[None, :]
    common = row_ids & col_ids
    parity = jnp.zeros((order, order), jnp.int32)
    for section_bit in range(max(order.bit_length() - 1, 0)):
        parity = parity + (common >> section_bit & 1)
    return (1 - 2 * (parity % 2)).astype(jnp.float32)


def per_device(x_tokens, sign_bits, weight, upstream):
    panel_width = x_tokens.shape[1]
    groups = lax.axis_size("tensor")
    factor = 1.0 / math.sqrt(panel_width * groups)
    column_sign = (1 - 2 * sign_bits).astype(jnp.bfloat16)
    signed = x_tokens * column_sign[None, :]
    partial_rot = jnp.dot(
        signed, hadamard(panel_width).astype(jnp.bfloat16), preferred_element_type=jnp.float32
    )
    current = partial_rot
    position = lax.axis_index("tensor")
    for section_bit in range(groups.bit_length() - 1):
        partner = partner_2(current.astype(jnp.bfloat16), "tensor", section_bit).astype(
            current.dtype
        )
        upper_half = position >> section_bit & 1 == 1
        current = jnp.where(upper_half, partner - current, current + partner)
    quantized = (current * factor).astype(jnp.bfloat16)
    gathered = lax.all_gather(quantized, "dp", axis=0, tiled=True)
    selected = gathered
    projected = lax.psum_scatter(
        jnp.dot(selected, weight, preferred_element_type=jnp.float32).astype(jnp.bfloat16),
        "tensor",
        scatter_dimension=0,
        tiled=True,
    )
    selected = gathered
    weight_grad = lax.dot_general(
        selected,
        lax.all_gather(upstream, "tensor", axis=0, tiled=True),
        (((0,), (0,)), ((), ())),
        preferred_element_type=jnp.float32,
    )
    return (projected, weight_grad)


def solution(mesh):
    in_specs = (P("dp", "tensor"), P("tensor"), P("tensor", "dp"), P("tensor", "dp"))
    out_specs = (P("tensor", "dp"), P("tensor", "dp"))
    return jax.shard_map(
        per_device, mesh=mesh, in_specs=in_specs, out_specs=out_specs, check_vma=False
    )
```

profile of v0, /device:TPU:0, one launch (start us, length us, event | category | flops | bytes accessed | tf_op | source)
XLA Modules:
  0.0 239.4 jit_solution(9900168703353716631)
XLA Ops:
  7.2 0.0 all-gather.3.cloned.1.call-start
  7.2 0.7 subtract_convert_fusion
  7.9 27.8 %fusion.25 = (bf16[64,2048]{1,0:T(8,128)(2,1)S(1)}, f32[64,2048]{1,0:T(8,128)S(1)}) fusion(bf16[64,2048]{1,0:T(8,128)(2,1)} %param.4, bf16[2048]{0:T(1024)(128)(2,1)S(1)} %subtract_convert_fusion), kind=kOutput, calls=%fused_computation.33 | convolution fusion | flops 738459648 | bytes 1052672 | tf_op jit(solution)/shard_map/dot_general | solution.py:35
  35.8 3.1 %collective-permute-start = (bf16[64,2048]{1,0:T(8,128)(2,1)S(1)}, bf16[64,2048]{1,0:T(8,128)(2,1)S(1)}, u32[]{:S(2)}, u32[]{:S(2)}) collective-permute-start(bf16[64,2048]{1,0:T(8,128)(2,1)S(1)} %get-tuple-element.2), channel_id=1, source_target_pairs={{0,1},{1,0},{2,3},{3,2},{4,5},{5,4},{6,7},{7,6},{8,9},{9,8},{10,11... | collective-permute-start | bytes 786440 | tf_op jit(solution)/shard_map/ppermute | solution.py:16
  38.9 6.3 %collective-permute-done = bf16[64,2048]{1,0:T(8,128)(2,1)S(1)} collective-permute-done((bf16[64,2048]{1,0:T(8,128)(2,1)S(1)}, bf16[64,2048]{1,0:T(8,128)(2,1)S(1)}, u32[]{:S(2)}, u32[]{:S(2)}) %collective-permute-start) | collective-permute-done | bytes 262176 | tf_op jit(solution)/shard_map/ppermute | solution.py:16
  45.2 0.1 fusion.11
  45.2 2.8 %collective-permute-start.1 = (bf16[64,2048]{1,0:T(8,128)(2,1)S(1)}, bf16[64,2048]{1,0:T(8,128)(2,1)S(1)}, u32[]{:S(2)}, u32[]{:S(2)}) collective-permute-start(bf16[64,2048]{1,0:T(8,128)(2,1)S(1)} %fusion.11), channel_id=1, source_target_pairs={{0,2},{2,0},{1,3},{3,1},{4,6},{6,4},{5,7},{7,5},{8,10},{10,8},{9,1... | collective-permute-start | bytes 786440 | tf_op jit(solution)/shard_map/ppermute | solution.py:16
  48.1 11.3 %collective-permute-done.1 = bf16[64,2048]{1,0:T(8,128)(2,1)S(1)} collective-permute-done((bf16[64,2048]{1,0:T(8,128)(2,1)S(1)}, bf16[64,2048]{1,0:T(8,128)(2,1)S(1)}, u32[]{:S(2)}, u32[]{:S(2)}) %collective-permute-start.1) | collective-permute-done | bytes 262176 | tf_op jit(solution)/shard_map/ppermute | solution.py:16
  59.3 0.9 fusion.10
  60.2 0.0 all-gather.3.cloned.1.call-update
  60.2 0.0 all-gather.5.cloned.1.call-start
  60.3 0.7 all-gather.5.cloned.1.call-update
  61.0 0.0 reduce-scatter.2.cloned.1.call-start
  61.0 28.2 %all-gather.3.cloned.1.call-done = bf16[512,2048]{1,0:T(8,128)(2,1)} async-done(((bf16[64,2048]{1,0:T(8,128)(2,1)}), bf16[512,2048]{1,0:T(8,128)(2,1)}) %all-gather.3.cloned.1.call-update) | async-done | bytes 2097168 | tf_op jit(solution)/shard_map/all_gather | solution.py:47
  89.2 0.0 copy-start
  89.2 14.9 %convolution_convert_fusion = bf16[512,3584]{1,0:T(8,128)(2,1)} fusion(bf16[512,2048]{1,0:T(8,128)(2,1)} %all-gather.3.cloned.1.call-done, bf16[2048,3584]{1,0:T(8,128)(2,1)} %param.6), kind=kOutput, calls=%fused_computation.9 | convolution fusion | flops 7518027776 | bytes 20447232 | tf_op jit(solution)/shard_map/dot_general | solution.py:50
  104.1 0.0 reduce-scatter.2.cloned.1.call-update
  104.2 58.8 %all-gather.5.cloned.1.call-done = bf16[512,3584]{1,0:T(8,128)(2,1)} async-done(((bf16[128,3584]{1,0:T(8,128)(2,1)}), bf16[512,3584]{1,0:T(8,128)(2,1)}) %all-gather.5.cloned.1.call-update) | async-done | bytes 3670032 | tf_op jit(solution)/shard_map/all_gather | solution.py:58
  163.0 0.0 copy-done
  163.0 16.4 %fusion.26 = f32[2048,3584]{1,0:T(8,128)} fusion(bf16[512,2048]{1,0:T(8,128)(2,1)S(1)} %copy-done, bf16[512,3584]{1,0:T(8,128)(2,1)} %all-gather.5.cloned.1.call-done), kind=kOutput, calls=%fused_computation.34 | convolution fusion | flops 7516192768 | bytes 35127296 | tf_op jit(solution)/shard_map/dot_general | solution.py:56
  179.3 53.6 %reduce-scatter.2.cloned.1.call-done = bf16[128,3584]{1,0:T(8,128)(2,1)} async-done(((bf16[512,3584]{1,0:T(8,128)(2,1)}), bf16[128,3584]{1,0:T(8,128)(2,1)}) %reduce-scatter.2.cloned.1.call-update) | async-done | bytes 917520 | tf_op jit(solution)/shard_map/reduce_scatter | solution.py:49
Async XLA Ops:
  7.2 82.1 %all-gather.3.cloned.1.call-start = ((), (), s32[]{:S(2)}) async-start(), calls=%async_computation.1 | async-start | bytes 2359296 | tf_op jit(solution)/shard_map/all_gather | solution.py:47
  35.8 9.4 %collective-permute-start = (bf16[64,2048]{1,0:T(8,128)(2,1)S(1)}, bf16[64,2048]{1,0:T(8,128)(2,1)S(1)}, u32[]{:S(2)}, u32[]{:S(2)}) collective-permute-start(bf16[64,2048]{1,0:T(8,128)(2,1)S(1)} %get-tuple-element.2), channel_id=1, source_target_pairs={{0,1},{1,0},{2,3},{3,2},{4,5},{5,4},{6,7},{7,6},{8,9},{9,8},{10,11... | collective-permute-start | bytes 786440 | tf_op jit(solution)/shard_map/ppermute | solution.py:16
  45.2 14.1 %collective-permute-start.1 = (bf16[64,2048]{1,0:T(8,128)(2,1)S(1)}, bf16[64,2048]{1,0:T(8,128)(2,1)S(1)}, u32[]{:S(2)}, u32[]{:S(2)}) collective-permute-start(bf16[64,2048]{1,0:T(8,128)(2,1)S(1)} %fusion.11), channel_id=1, source_target_pairs={{0,2},{2,0},{1,3},{3,1},{4,6},{6,4},{5,7},{7,5},{8,10},{10,8},{9,1... | collective-permute-start | bytes 786440 | tf_op jit(solution)/shard_map/ppermute | solution.py:16
  60.2 102.8 %all-gather.5.cloned.1.call-start = ((), (), s32[]{:S(2)}) async-start(), calls=%async_computation.3 | async-start | bytes 4587520 | tf_op jit(solution)/shard_map/all_gather | solution.py:58
  61.0 171.9 %reduce-scatter.2.cloned.1.call-start = ((), (), s32[]{:S(2)}) async-start(), calls=%async_computation.2 | async-start | bytes 4587520 | tf_op jit(solution)/shard_map/reduce_scatter | solution.py:49
  89.2 73.7 %copy-start = (bf16[512,2048]{1,0:T(8,128)(2,1)S(1)}, bf16[512,2048]{1,0:T(8,128)(2,1)}, u32[]{:S(2)}) copy-start(bf16[512,2048]{1,0:T(8,128)(2,1)} %all-gather.3.cloned.1.call-done) | copy-start | bytes 6291460
Sparse Core Ops, SparseCore 0:
  60.3 28.8 all-gather.2
  90.8 72.1 all-gather.4
  165.8 66.9 reduce-scatter.1
where the time goes:
time: 240 us; the launch traced here: 239 us
  waiting for transfers between devices  159 us (66%)
  matrix products  59.1 us (25%)
  between operations  13.8 us (6%)
  starting transfers between devices  6.03 us (3%)
    all_gather x1, waiting for transfers between devices, per_device(): lax.all_gather(upstream, 'tensor', axis=0, tiled=True)  58.8 us
    reduce_scatter x1, waiting for transfers between devices, per_device(): lax.psum_scatter(jnp.dot(selected, weight, preferred_element_type=jnp.flo...  53.6 us
    all_gather x1, waiting for transfers between devices, per_device(): gathered = lax.all_gather(quantized, 'dp', axis=0, tiled=True)  28.2 us
    dot_general x1, matrix products, per_device(): jnp.dot(signed, hadamard(panel_width).astype(jnp.bfloat16), preferred_ele...  27.8 us
    ppermute x2, waiting for transfers between devices, partner_2(): return lax.ppermute(block, axis, route)  17.6 us
    dot_general x1, matrix products, per_device(): lax.dot_general(selected, lax.all_gather(upstream, 'tensor', axis=0, tile...  16.4 us
    dot_general x1, matrix products, per_device(): jnp.dot(selected, weight, preferred_element_type=jnp.float32)  14.9 us
    ppermute x2, starting transfers between devices, partner_2(): return lax.ppermute(block, axis, route)  5.91 us
  transfers between devices with their start and end apart: 5, of which 5 were waited for; matrix products, arithmetic and copies ran while one was open for 13% of the time, Pallas kernels for 0%

commit v1 on v0

v1 whole, which is shorter than its diff:
```python
import functools
import math

import jax
import jax.numpy as jnp
from jax import lax
from jax.experimental import pallas as pl
from jax.experimental.pallas import tpu as pltpu
from jax.sharding import PartitionSpec as P

MIB = 1 << 20


def parity_sign(bits):
    folded = bits ^ (bits >> 4)
    folded = folded ^ (folded >> 2)
    folded = folded ^ (folded >> 1)
    return (1 - 2 * (folded & 1)).astype(jnp.float32)


def hadamard(order):
    row_ids = jnp.arange(order, dtype=jnp.int32)[:, None]
    col_ids = jnp.arange(order, dtype=jnp.int32)[None, :]
    common = row_ids & col_ids
    parity = jnp.zeros((order, order), jnp.int32)
    for section_bit in range(max(order.bit_length() - 1, 0)):
        parity = parity + (common >> section_bit & 1)
    return (1 - 2 * (parity % 2)).astype(jnp.bfloat16)


def butterfly(parts):
    stride = 1
    parts = list(parts)
    while stride < len(parts):
        for low in range(len(parts)):
            if not low & stride:
                a, b = parts[low], parts[low | stride]
                parts[low], parts[low | stride] = a + b, a - b
        stride *= 2
    return parts


def rotate_kernel(groups, core_order, factor, z_ref, h_ref, *refs):
    pieces, outs = refs[:groups], refs[groups:]
    z = z_ref[0]
    width = pieces[0].shape[1]
    h = h_ref[...]
    rotated = []
    for i, piece in enumerate(pieces):
        sign = parity_sign(z & i)
        chunks = [
            jnp.dot(
                piece[:, j * core_order : (j + 1) * core_order],
                h,
                preferred_element_type=jnp.float32,
            )
            * sign
            for j in range(width // core_order)
        ]
        rotated.append(butterfly(chunks))
    for j in range(width // core_order):
        panel = butterfly([r[j] for r in rotated])
        for m in range(groups):
            scale = parity_sign((z ^ m) & z) * factor
            outs[m][:, j * core_order : (j + 1) * core_order] = (panel[m] * scale).astype(
                jnp.bfloat16
            )


def rotate(z, pieces):
    groups = len(pieces)
    rows, width = pieces[0].shape
    core_order = min(256, width)
    vmem = pl.BlockSpec(memory_space=pltpu.VMEM)
    return pl.pallas_call(
        functools.partial(
            rotate_kernel, groups, core_order, 1.0 / math.sqrt(width * groups)
        ),
        out_shape=[jax.ShapeDtypeStruct((rows, width), jnp.bfloat16)] * groups,
        in_specs=[pl.BlockSpec(memory_space=pltpu.SMEM)] + [vmem] * (groups + 1),
        out_specs=[vmem] * groups,
        name="rotate",
    )(z.reshape(1), hadamard(core_order), *pieces)


def place_kernel(span, group_rows, where_ref, *refs):
    pieces, out = refs[:-1], refs[-1]
    for n, piece in enumerate(pieces):
        for i in range(piece.shape[0] // group_rows):
            start = pl.multiple_of(where_ref[n, i], group_rows)
            out[pl.ds(start, group_rows), :] = piece[i * group_rows : (i + 1) * group_rows, :]


def place(pieces, starts, group_rows):
    total = sum(p.shape[0] for p in pieces)
    width = pieces[0].shape[1]
    if group_rows % 16:
        groups = total // group_rows
        stacked = jnp.concatenate(pieces).reshape(groups, group_rows, width)
        order = jnp.zeros((groups,), jnp.int32).at[starts.reshape(-1) // group_rows].set(
            jnp.arange(groups, dtype=jnp.int32)
        )
        return jnp.take(stacked, order, axis=0).reshape(total, width)
    vmem = pl.BlockSpec(memory_space=pltpu.VMEM)
    return pl.pallas_call(
        functools.partial(place_kernel, total, group_rows),
        out_shape=jax.ShapeDtypeStruct((total, width), jnp.bfloat16),
        in_specs=[pl.BlockSpec(memory_space=pltpu.SMEM)] + [vmem] * len(pieces),
        out_specs=vmem,
        compiler_params=pltpu.CompilerParams(vmem_limit_bytes=32 * MIB),
        name="place",
    )(starts, *pieces)


def project_kernel(q_ref, w_ref, out_ref):
    out_ref[...] = jnp.dot(
        q_ref[...], w_ref[...], preferred_element_type=jnp.float32
    ).astype(out_ref.dtype)


def project(q, weight, first, width):
    tile = next((t for t in (512, 256, 128) if width % t == 0 and first % t == 0), width)
    tokens, depth = q.shape
    return pl.pallas_call(
        project_kernel,
        out_shape=jax.ShapeDtypeStruct((tokens, width), jnp.bfloat16),
        grid=(width // tile,),
        in_specs=[
            pl.BlockSpec((tokens, depth), lambda n: (0, 0)),
            pl.BlockSpec((depth, tile), lambda n: (0, n + first // tile)),
        ],
        out_specs=pl.BlockSpec((tokens, tile), lambda n: (0, n)),
        compiler_params=pltpu.CompilerParams(vmem_limit_bytes=48 * MIB),
        cost_estimate=pl.CostEstimate(
            flops=2 * tokens * depth * width,
            bytes_accessed=2 * (tokens * depth + depth * width + tokens * width),
            transcendentals=0,
        ),
        name="project",
    )(q, weight)


def swap(block, axis, mask):
    count = lax.axis_size(axis)
    return lax.ppermute(block, axis, [(i, i ^ mask) for i in range(count)])


def gather_rows(block, axis, orders):
    step = block.shape[0] // len(orders)
    held = []
    for part, order in enumerate(orders):
        have = [(0, part, block[part * step : (part + 1) * step])]
        for bit in order:
            have += [(mask | bit, part, swap(array, axis, bit)) for mask, part, array in have]
        held += have
    return held


def shift(block, axis, pairs):
    return lax.ppermute(block, axis, pairs)


def scatter_sum(partial, z, groups):
    rows = partial.shape[0] // groups

    def block(index):
        return lax.dynamic_slice_in_dim(
            partial, jnp.clip(index, 0, groups - 1) * rows, rows, axis=0
        ).astype(jnp.float32)

    up = down = None
    for s in range(1, groups):
        send_up, send_down = block(z + groups - s), block(z - groups + s)
        if s > 1:
            send_up, send_down = send_up + up, send_down + down
        up = shift(
            send_up.astype(jnp.bfloat16), "tensor", [(i, i + 1) for i in range(s)]
        ).astype(jnp.float32)
        down = shift(
            send_down.astype(jnp.bfloat16),
            "tensor",
            [(i, i - 1) for i in range(groups - s, groups)],
        ).astype(jnp.float32)
    return (block(z) + up + down).astype(jnp.bfloat16)


def per_device(x_tokens, sign_bits, weight, upstream):
    groups = lax.axis_size("tensor")
    ways = lax.axis_size("dp")
    z = lax.axis_index("tensor")
    d = lax.axis_index("dp")
    rows, panel = x_tokens.shape
    hidden = weight.shape[1]
    group_rows = rows // groups

    all_up = lax.all_gather(upstream, "tensor", axis=0, tiled=True)

    column_sign = (1 - 2 * sign_bits).astype(jnp.bfloat16)
    signed = x_tokens * column_sign[None, :]
    pieces = []
    for m in range(groups):
        piece = lax.dynamic_slice_in_dim(signed, (z ^ m) * group_rows, group_rows, axis=0)
        pieces.append(swap(piece, "tensor", m) if m else piece)
    turned = rotate(z, pieces)
    back = [swap(t, "tensor", m) if m else t for m, t in enumerate(turned)]

    bits = [1 << b for b in range(1, ways.bit_length() - 1)]
    half = len(bits) // 2
    orders = [bits + [1], bits[half:] + bits[:half] + [1]]
    own = jnp.concatenate(back)
    held = gather_rows(own, "dp", orders)
    per_part = groups // len(orders)
    starts = jnp.stack(
        [
            jnp.stack(
                [(d ^ mask) * rows + (z ^ (part * per_part + i)) * group_rows for i in range(per_part)]
            )
            for mask, part, _ in held
        ]
    ).astype(jnp.int32)
    q = place([array for _, _, array in held], starts, group_rows)

    cuts = 2 if hidden % 512 == 0 else 1
    width = hidden // cuts
    projected = jnp.concatenate(
        [
            scatter_sum(project(q, weight, c * width, width), z, groups)
            for c in range(cuts)
        ],
        axis=1,
    )
    weight_grad = lax.dot_general(
        q, all_up, (((0,), (0,)), ((), ())), preferred_element_type=jnp.float32
    )
    return (projected, weight_grad)


def solution(mesh):
    in_specs = (P("dp", "tensor"), P("tensor"), P("tensor", "dp"), P("tensor", "dp"))
    out_specs = (P("tensor", "dp"), P("tensor", "dp"))
    return jax.shard_map(
        per_device, mesh=mesh, in_specs=in_specs, out_specs=out_specs, check_vma=False
    )
```

time: 240 us -> 187 us (0.78)
  the two profiles are of different devices: /device:TPU:0 before, /device:TPU:10 now
where the time goes in v1:
time: 187 us; the launch traced here: 186 us
  waiting for transfers between devices  84.1 us (45%)
  starting transfers between devices  36.4 us (19%)
  Pallas kernels  19 us (10%)
  matrix products  16.4 us (9%)
  between operations  14.3 us (8%)
  local copies, waits for them, and re-layouts  10.1 us (5%)
  other arithmetic  5.48 us (3%)
    ppermute x12, waiting for transfers between devices, shift(): return lax.ppermute(block, axis, pairs)  59.6 us
    ppermute x20, waiting for transfers between devices, swap(): return lax.ppermute(block, axis, [(i, i ^ mask) for i in range(count)])  24.5 us
    ppermute x12, starting transfers between devices, shift(): return lax.ppermute(block, axis, pairs)  23.3 us
    dot_general x1, matrix products, per_device(): lax.dot_general(q, all_up, (((0,), (0,)), ((), ())), preferred_element_ty...  16.4 us
    pallas_call x2, Pallas kernels, project(): pl.pallas_call(project_kernel, out_shape=jax.ShapeDtypeStruct((tokens, wi...  15.8 us
    ppermute x20, starting transfers between devices, swap(): return lax.ppermute(block, axis, [(i, i ^ mask) for i in range(count)])  13 us
    unnamed x28, local copies, waits for them, and re-layouts  9.26 us
  transfers between devices with their start and end apart: 33, of which 16 were waited for; matrix products, arithmetic and copies ran while one was open for 3% of the time, Pallas kernels for 10%

profile of v1, /device:TPU:10, one launch (start us, length us, event | category | flops | bytes accessed | tf_op | source)
XLA Modules:
  0.0 185.8 jit_solution(3359691598200765028)
XLA Ops:
  7.2 0.7 subtract_convert_fusion
  7.9 1.0 broadcast_multiply_fusion
  8.9 0.7 constant_dynamic-slice_fusion.4
  9.6 0.4 collective-permute-start
  10.0 2.6 %collective-permute-start.1 = (bf16[16,2048]{1,0:T(8,128)(2,1)S(1)}, bf16[16,2048]{1,0:T(8,128)(2,1)S(1)}, u32[]{:S(2)}, u32[]{:S(2)}) collective-permute-start(bf16[16,2048]{1,0:T(8,128)(2,1)S(1)} %get-tuple-element.19), channel_id=1, source_target_pairs={{0,2},{1,3},{2,0},{3,1},{4,6},{5,7},{6,4},{7,5},{8,10},{9,11},{10,... | collective-permute-start | bytes 196616 | tf_op jit(solution)/shard_map/ppermute | solution.py:145
  12.6 0.5 collective-permute-start.2
  13.1 1.0 fusion.3.h_ref
  14.2 3.0 %collective-permute-done.1.refs_2_ = bf16[16,2048]{1,0:T(8,128)(2,1)S(1)} collective-permute-done((bf16[16,2048]{1,0:T(8,128)(2,1)S(1)}, bf16[16,2048]{1,0:T(8,128)(2,1)S(1)}, u32[]{:S(2)}, u32[]{:S(2)}) %collective-permute-start.1) | collective-permute-done | bytes 65568 | tf_op jit(solution)/shard_map/ppermute | solution.py:145
  17.2 0.9 collective-permute-done.2.refs_3_
  18.1 0.6 copy-done.12
  18.7 2.4 %rotate.1 = (bf16[16,2048]{1,0:T(8,128)(2,1)}, bf16[16,2048]{1,0:T(8,128)(2,1)}, bf16[16,2048]{1,0:T(8,128)(2,1)}, bf16[16,2048]{1,0:T(8,128)(2,1)}) custom-call(s32[1]{0:T(128)} %bitcast.48.z_ref, bf16[256,256]{1,0:T(8,128)(2,1)} %fusion.3.h_ref, bf16[16,2048]{1,0:T(8,128)(2,1)} %get-tuple-element.21.refs_0_, bf16[16,2048]{1,0:T(8,128)(2,1)} %copy-done.10, ...), custom_call_target="tpu_custom_call" | custom-call | tf_op jit(solution)/shard_map/rotate/pallas_call | solution.py:75
  21.2 2.5 %collective-permute-start.11 = (bf16[16,2048]{1,0:T(8,128)(2,1)}, bf16[16,2048]{1,0:T(8,128)(2,1)S(1)}, u32[]{:S(2)}, u32[]{:S(2)}) collective-permute-start(bf16[16,2048]{1,0:T(8,128)(2,1)} %get-tuple-element.8), channel_id=1, source_target_pairs={{0,2},{1,3},{2,0},{3,1},{4,6},{5,7},{6,4},{7,5},{8,10},{9,11},{10,... | collective-permute-start | bytes 196616 | tf_op jit(solution)/shard_map/ppermute | solution.py:145
  23.7 1.1 collective-permute-start.12
  24.8 0.9 constant_dynamic-update-slice_fusion.1
  25.6 0.8 collective-permute-start.3
  26.4 4.5 %collective-permute-done.11 = bf16[16,2048]{1,0:T(8,128)(2,1)S(1)} collective-permute-done((bf16[16,2048]{1,0:T(8,128)(2,1)}, bf16[16,2048]{1,0:T(8,128)(2,1)S(1)}, u32[]{:S(2)}, u32[]{:S(2)}) %collective-permute-start.11) | collective-permute-done | bytes 65568 | tf_op jit(solution)/shard_map/ppermute | solution.py:145
  30.9 6.2 %collective-permute-done.12 = bf16[16,2048]{1,0:T(8,128)(2,1)S(1)} collective-permute-done((bf16[16,2048]{1,0:T(8,128)(2,1)}, bf16[16,2048]{1,0:T(8,128)(2,1)S(1)}, u32[]{:S(2)}, u32[]{:S(2)}) %collective-permute-start.12) | collective-permute-done | bytes 65568 | tf_op jit(solution)/shard_map/ppermute | solution.py:145
  37.1 1.5 collective-permute-start.13
  38.6 0.5 collective-permute-start.14
  39.2 1.6 collective-permute-start.4
  40.9 0.5 collective-permute-start.5
  41.4 0.7 collective-permute-done.13.refs_9_
  42.1 2.8 %collective-permute-done.14.refs_10_ = bf16[32,2048]{1,0:T(8,128)(2,1)S(1)} collective-permute-done((bf16[32,2048]{1,0:T(8,128)(2,1)S(1)}, bf16[32,2048]{1,0:T(8,128)(2,1)S(1)}, u32[]{:S(2)}, u32[]{:S(2)}) %collective-permute-start.14) | collective-permute-done | bytes 131104 | tf_op jit(solution)/shard_map/ppermute | solution.py:145
  44.9 2.7 %collective-permute-done.4.refs_1_ = bf16[32,2048]{1,0:T(8,128)(2,1)S(1)} collective-permute-done((bf16[32,2048]{1,0:T(8,128)(2,1)S(1)}, bf16[32,2048]{1,0:T(8,128)(2,1)S(1)}, u32[]{:S(2)}, u32[]{:S(2)}) %collective-permute-start.4) | collective-permute-done | bytes 131104 | tf_op jit(solution)/shard_map/ppermute | solution.py:145
  47.8 0.5 collective-permute-start.18
  48.2 1.6 collective-permute-done.15.refs_11_
  49.8 0.5 collective-permute-start.19
  50.3 2.2 %collective-permute-done.6.refs_3_ = bf16[32,2048]{1,0:T(8,128)(2,1)S(1)} collective-permute-done((bf16[32,2048]{1,0:T(8,128)(2,1)S(1)}, bf16[32,2048]{1,0:T(8,128)(2,1)S(1)}, u32[]{:S(2)}, u32[]{:S(2)}) %collective-permute-start.6) | collective-permute-done | bytes 131104 | tf_op jit(solution)/shard_map/ppermute | solution.py:145
  52.8 0.6 copy-done.2
  53.4 0.7 copy-done
  54.1 0.7 copy-done.4
  54.7 0.6 copy-done.6
  55.4 0.7 copy-done.8
  56.0 0.9 copy-done.1
  56.9 0.9 copy-done.3
  57.8 0.9 copy-done.5
  58.7 0.9 copy-done.7
  59.6 0.9 copy-done.9
  60.6 0.8 place.1.q_ref
  61.4 7.9 %project.2 = bf16[512,1792]{1,0:T(8,128)(2,1)S(1)} custom-call(bf16[512,2048]{1,0:T(8,128)(2,1)S(1)} %place.1.q_ref, bf16[2048,3584]{1,0:T(8,128)(2,1)} %w_ref.3), custom_call_target="tpu_custom_call" | custom-call | flops 3758096384 | bytes 11272192 | tf_op jit(solution)/shard_map/project/pallas_call | solution.py:124
  69.3 1.3 collective-permute-start.20
  70.6 0.7 collective-permute-start.23
  71.3 7.9 %project.3 = bf16[512,1792]{1,0:T(8,128)(2,1)S(1)} custom-call(bf16[512,2048]{1,0:T(8,128)(2,1)S(1)} %place.1.q_ref, bf16[2048,3584]{1,0:T(8,128)(2,1)} %w_ref.3), custom_call_target="tpu_custom_call" | custom-call | flops 3758096384 | bytes 11272192 | tf_op jit(solution)/shard_map/project/pallas_call | solution.py:124
  79.3 1.3 collective-permute-start.26
  80.6 0.7 collective-permute-start.29
  81.3 13.1 %collective-permute-done.20 = bf16[128,1792]{1,0:T(8,128)(2,1)S(1)} collective-permute-done((bf16[128,1792]{1,0:T(8,128)(2,1)S(1)}, bf16[128,1792]{1,0:T(8,128)(2,1)S(1)}, u32[]{:S(2)}, u32[]{:S(2)}) %collective-permute-start.20) | collective-permute-done | bytes 458784 | tf_op jit(solution)/shard_map/ppermute | solution.py:160
  94.5 1.9 %collective-permute-start.21 = (bf16[128,1792]{1,0:T(8,128)(2,1)S(1)}, bf16[128,1792]{1,0:T(8,128)(2,1)S(1)}, u32[]{:S(2)}, u32[]{:S(2)}) collective-permute-start(bf16[128,1792]{1,0:T(8,128)(2,1)S(1)} %add_convert_fusion.9), channel_id=1, source_target_pairs={{0,1},{1,2},{4,5},{5,6},{8,9},{9,10},{12,13},{13,14},{16,17},{17,1... | collective-permute-start | bytes 1376264 | tf_op jit(solution)/shard_map/ppermute | solution.py:160
  96.5 11.3 %collective-permute-done.26 = bf16[128,1792]{1,0:T(8,128)(2,1)S(1)} collective-permute-done((bf16[128,1792]{1,0:T(8,128)(2,1)S(1)}, bf16[128,1792]{1,0:T(8,128)(2,1)S(1)}, u32[]{:S(2)}, u32[]{:S(2)}) %collective-permute-start.26) | collective-permute-done | bytes 458784 | tf_op jit(solution)/shard_map/ppermute | solution.py:160
  107.8 1.9 %collective-permute-start.27 = (bf16[128,1792]{1,0:T(8,128)(2,1)S(1)}, bf16[128,1792]{1,0:T(8,128)(2,1)S(1)}, u32[]{:S(2)}, u32[]{:S(2)}) collective-permute-start(bf16[128,1792]{1,0:T(8,128)(2,1)S(1)} %add_convert_fusion.4), channel_id=1, source_target_pairs={{0,1},{1,2},{4,5},{5,6},{8,9},{9,10},{12,13},{13,14},{16,17},{17,1... | collective-permute-start | bytes 1376264 | tf_op jit(solution)/shard_map/ppermute | solution.py:160
  109.8 7.8 %collective-permute-done.21 = bf16[128,1792]{1,0:T(8,128)(2,1)S(1)} collective-permute-done((bf16[128,1792]{1,0:T(8,128)(2,1)S(1)}, bf16[128,1792]{1,0:T(8,128)(2,1)S(1)}, u32[]{:S(2)}, u32[]{:S(2)}) %collective-permute-start.21) | collective-permute-done | bytes 458784 | tf_op jit(solution)/shard_map/ppermute | solution.py:160
  117.6 0.2 add_convert_fusion.8
  117.8 1.3 collective-permute-start.24
  119.1 4.6 %collective-permute-start.22 = (bf16[128,1792]{1,0:T(8,128)(2,1)S(1)}, bf16[128,1792]{1,0:T(8,128)(2,1)S(1)}, u32[]{:S(2)}, u32[]{:S(2)}) collective-permute-start(bf16[128,1792]{1,0:T(8,128)(2,1)S(1)} %get-tuple-element.10), channel_id=1, source_target_pairs={{0,1},{1,2},{2,3},{4,5},{5,6},{6,7},{8,9},{9,10},{10,11},{12,13},{... | collective-permute-start | bytes 1376264 | tf_op jit(solution)/shard_map/ppermute | solution.py:160
  123.7 3.7 %collective-permute-done.27 = bf16[128,1792]{1,0:T(8,128)(2,1)S(1)} collective-permute-done((bf16[128,1792]{1,0:T(8,128)(2,1)S(1)}, bf16[128,1792]{1,0:T(8,128)(2,1)S(1)}, u32[]{:S(2)}, u32[]{:S(2)}) %collective-permute-start.27) | collective-permute-done | bytes 458784 | tf_op jit(solution)/shard_map/ppermute | solution.py:160
  127.4 0.2 add_convert_fusion.3
  127.6 1.3 collective-permute-start.30
  128.9 4.6 %collective-permute-start.28 = (bf16[128,1792]{1,0:T(8,128)(2,1)S(1)}, bf16[128,1792]{1,0:T(8,128)(2,1)S(1)}, u32[]{:S(2)}, u32[]{:S(2)}) collective-permute-start(bf16[128,1792]{1,0:T(8,128)(2,1)S(1)} %get-tuple-element.14), channel_id=1, source_target_pairs={{0,1},{1,2},{2,3},{4,5},{5,6},{6,7},{8,9},{9,10},{10,11},{12,13},{... | collective-permute-start | bytes 1376264 | tf_op jit(solution)/shard_map/ppermute | solution.py:160
  133.6 1.9 %collective-permute-start.25 = (bf16[128,1792]{1,0:T(8,128)(2,1)S(1)}, bf16[128,1792]{1,0:T(8,128)(2,1)S(1)}, u32[]{:S(2)}, u32[]{:S(2)}) collective-permute-start(bf16[128,1792]{1,0:T(8,128)(2,1)S(1)} %add_convert_fusion.6), channel_id=1, source_target_pairs={{1,0},{2,1},{3,2},{5,4},{6,5},{7,6},{9,8},{10,9},{11,10},{13,12},{... | collective-permute-start | bytes 1376264 | tf_op jit(solution)/shard_map/ppermute | solution.py:160
  135.5 7.4 %collective-permute-done.30 = bf16[128,1792]{1,0:T(8,128)(2,1)S(1)} collective-permute-done((bf16[128,1792]{1,0:T(8,128)(2,1)S(1)}, bf16[128,1792]{1,0:T(8,128)(2,1)S(1)}, u32[]{:S(2)}, u32[]{:S(2)}) %collective-permute-start.30) | collective-permute-done | bytes 458784 | tf_op jit(solution)/shard_map/ppermute | solution.py:160
  143.0 1.9 %collective-permute-start.31 = (bf16[128,1792]{1,0:T(8,128)(2,1)S(1)}, bf16[128,1792]{1,0:T(8,128)(2,1)S(1)}, u32[]{:S(2)}, u32[]{:S(2)}) collective-permute-start(bf16[128,1792]{1,0:T(8,128)(2,1)S(1)} %add_convert_fusion.1), channel_id=1, source_target_pairs={{1,0},{2,1},{3,2},{5,4},{6,5},{7,6},{9,8},{10,9},{11,10},{13,12},{... | collective-permute-start | bytes 1376264 | tf_op jit(solution)/shard_map/ppermute | solution.py:160
  145.0 7.8 %collective-permute-done.25 = bf16[128,1792]{1,0:T(8,128)(2,1)S(1)} collective-permute-done((bf16[128,1792]{1,0:T(8,128)(2,1)S(1)}, bf16[128,1792]{1,0:T(8,128)(2,1)S(1)}, u32[]{:S(2)}, u32[]{:S(2)}) %collective-permute-start.25) | collective-permute-done | bytes 458784 | tf_op jit(solution)/shard_map/ppermute | solution.py:160
  152.9 8.5 %collective-permute-done.31 = bf16[128,1792]{1,0:T(8,128)(2,1)S(1)} collective-permute-done((bf16[128,1792]{1,0:T(8,128)(2,1)S(1)}, bf16[128,1792]{1,0:T(8,128)(2,1)S(1)}, u32[]{:S(2)}, u32[]{:S(2)}) %collective-permute-start.31) | collective-permute-done | bytes 458784 | tf_op jit(solution)/shard_map/ppermute | solution.py:160
  161.6 1.0 pad_maximum_fusion
  162.6 16.4 %fusion.4 = f32[2048,3584]{1,0:T(8,128)} fusion(bf16[512,2048]{1,0:T(8,128)(2,1)S(1)} %place.1.q_ref, bf16[512,3584]{1,0:T(8,128)(2,1)} %all-gather.2.cloned.1.call-done), kind=kOutput, calls=%fused_computation.48 | convolution fusion | flops 7516192768 | bytes 35127296 | tf_op jit(solution)/shard_map/dot_general | solution.py:232
  (62 shorter events, 1.8 us)
Async XLA Ops:
  7.2 155.4 %all-gather.2.cloned.1.call-start = ((), (), s32[]{:S(2)}) async-start(), calls=%async_computation | async-start | bytes 4587520 | tf_op jit(solution)/shard_map/all_gather | solution.py:196
  9.6 4.7 %collective-permute-start = (bf16[16,2048]{1,0:T(8,128)(2,1)S(1)}, bf16[16,2048]{1,0:T(8,128)(2,1)S(1)}, u32[]{:S(2)}, u32[]{:S(2)}) collective-permute-start(bf16[16,2048]{1,0:T(8,128)(2,1)S(1)} %get-tuple-element.20), channel_id=1, source_target_pairs={{0,1},{1,0},{2,3},{3,2},{4,5},{5,4},{6,7},{7,6},{8,9},{9,8},{10,11... | collective-permute-start | bytes 196616 | tf_op jit(solution)/shard_map/ppermute | solution.py:145
  10.0 7.2 %collective-permute-start.1 = (bf16[16,2048]{1,0:T(8,128)(2,1)S(1)}, bf16[16,2048]{1,0:T(8,128)(2,1)S(1)}, u32[]{:S(2)}, u32[]{:S(2)}) collective-permute-start(bf16[16,2048]{1,0:T(8,128)(2,1)S(1)} %get-tuple-element.19), channel_id=1, source_target_pairs={{0,2},{1,3},{2,0},{3,1},{4,6},{5,7},{6,4},{7,5},{8,10},{9,11},{10,... | collective-permute-start | bytes 196616 | tf_op jit(solution)/shard_map/ppermute | solution.py:145
  12.6 5.5 %collective-permute-start.2 = (bf16[16,2048]{1,0:T(8,128)(2,1)S(1)}, bf16[16,2048]{1,0:T(8,128)(2,1)S(1)}, u32[]{:S(2)}, u32[]{:S(2)}) collective-permute-start(bf16[16,2048]{1,0:T(8,128)(2,1)S(1)} %get-tuple-element.18), channel_id=1, source_target_pairs={{0,3},{1,2},{2,1},{3,0},{4,7},{5,6},{6,5},{7,4},{8,11},{9,10},{10,... | collective-permute-start | bytes 196616 | tf_op jit(solution)/shard_map/ppermute | solution.py:145
  14.2 3.9 %copy-start.10 = (bf16[16,2048]{1,0:T(8,128)(2,1)}, bf16[16,2048]{1,0:T(8,128)(2,1)S(1)}, u32[]{:S(2)}) copy-start(bf16[16,2048]{1,0:T(8,128)(2,1)S(1)} %collective-permute-done.refs_1_) | copy-start | bytes 196612
  17.2 0.9 copy-start.11
  18.1 0.6 copy-start.12
  21.2 9.7 %collective-permute-start.11 = (bf16[16,2048]{1,0:T(8,128)(2,1)}, bf16[16,2048]{1,0:T(8,128)(2,1)S(1)}, u32[]{:S(2)}, u32[]{:S(2)}) collective-permute-start(bf16[16,2048]{1,0:T(8,128)(2,1)} %get-tuple-element.8), channel_id=1, source_target_pairs={{0,2},{1,3},{2,0},{3,1},{4,6},{5,7},{6,4},{7,5},{8,10},{9,11},{10,... | collective-permute-start | bytes 196616 | tf_op jit(solution)/shard_map/ppermute | solution.py:145
  23.7 13.4 %collective-permute-start.12 = (bf16[16,2048]{1,0:T(8,128)(2,1)}, bf16[16,2048]{1,0:T(8,128)(2,1)S(1)}, u32[]{:S(2)}, u32[]{:S(2)}) collective-permute-start(bf16[16,2048]{1,0:T(8,128)(2,1)} %get-tuple-element.9), channel_id=1, source_target_pairs={{0,3},{1,2},{2,1},{3,0},{4,7},{5,6},{6,5},{7,4},{8,11},{9,10},{10,... | collective-permute-start | bytes 196616 | tf_op jit(solution)/shard_map/ppermute | solution.py:145
  25.6 13.5 %collective-permute-start.3 = (bf16[16,2048]{1,0:T(8,128)(2,1)}, bf16[16,2048]{1,0:T(8,128)(2,1)S(1)}, u32[]{:S(2)}, u32[]{:S(2)}) collective-permute-start(bf16[16,2048]{1,0:T(8,128)(2,1)} %get-tuple-element.7), channel_id=1, source_target_pairs={{0,1},{1,0},{2,3},{3,2},{4,5},{5,4},{6,7},{7,6},{8,9},{9,8},{10,11... | collective-permute-start | bytes 196616 | tf_op jit(solution)/shard_map/ppermute | solution.py:145
  37.1 5.0 %collective-permute-start.13 = (bf16[32,2048]{1,0:T(8,128)(2,1)S(1)}, bf16[32,2048]{1,0:T(8,128)(2,1)S(1)}, u32[]{:S(2)}, u32[]{:S(2)}) collective-permute-start(bf16[32,2048]{1,0:T(8,128)(2,1)S(1)} %constant_dynamic-update-slice_fusion.2.refs_8_), channel_id=1, source_target_pairs={{0,16},{4,20},{8,24},{12,28},{16,0},{20,4},{24,8},{28,12},{1,17},{... | collective-permute-start | bytes 393224 | tf_op jit(solution)/shard_map/ppermute | solution.py:145
  38.6 6.2 %collective-permute-start.14 = (bf16[32,2048]{1,0:T(8,128)(2,1)S(1)}, bf16[32,2048]{1,0:T(8,128)(2,1)S(1)}, u32[]{:S(2)}, u32[]{:S(2)}) collective-permute-start(bf16[32,2048]{1,0:T(8,128)(2,1)S(1)} %constant_dynamic-update-slice_fusion.2.refs_8_), channel_id=1, source_target_pairs={{0,8},{4,12},{8,0},{12,4},{16,24},{20,28},{24,16},{28,20},{1,9},{5... | collective-permute-start | bytes 393224 | tf_op jit(solution)/shard_map/ppermute | solution.py:145
  39.1 5.7 %collective-permute-start.16 = (bf16[32,2048]{1,0:T(8,128)(2,1)S(1)}, bf16[32,2048]{1,0:T(8,128)(2,1)S(1)}, u32[]{:S(2)}, u32[]{:S(2)}) collective-permute-start(bf16[32,2048]{1,0:T(8,128)(2,1)S(1)} %constant_dynamic-update-slice_fusion.2.refs_8_), channel_id=1, source_target_pairs={{0,4},{4,0},{8,12},{12,8},{16,20},{20,16},{24,28},{28,24},{1,5},{5... | collective-permute-start | bytes 393224 | tf_op jit(solution)/shard_map/ppermute | solution.py:145
  39.2 8.4 %collective-permute-start.4 = (bf16[32,2048]{1,0:T(8,128)(2,1)S(1)}, bf16[32,2048]{1,0:T(8,128)(2,1)S(1)}, u32[]{:S(2)}, u32[]{:S(2)}) collective-permute-start(bf16[32,2048]{1,0:T(8,128)(2,1)S(1)} %constant_dynamic-update-slice_fusion.refs_0_), channel_id=1, source_target_pairs={{0,8},{4,12},{8,0},{12,4},{16,24},{20,28},{24,16},{28,20},{1,9},{5... | collective-permute-start | bytes 393224 | tf_op jit(solution)/shard_map/ppermute | solution.py:145
  40.9 6.8 %collective-permute-start.5 = (bf16[32,2048]{1,0:T(8,128)(2,1)S(1)}, bf16[32,2048]{1,0:T(8,128)(2,1)S(1)}, u32[]{:S(2)}, u32[]{:S(2)}) collective-permute-start(bf16[32,2048]{1,0:T(8,128)(2,1)S(1)} %constant_dynamic-update-slice_fusion.refs_0_), channel_id=1, source_target_pairs={{0,16},{4,20},{8,24},{12,28},{16,0},{20,4},{24,8},{28,12},{1,17},{... | collective-permute-start | bytes 393224 | tf_op jit(solution)/shard_map/ppermute | solution.py:145
  42.1 5.7 %collective-permute-start.7 = (bf16[32,2048]{1,0:T(8,128)(2,1)S(1)}, bf16[32,2048]{1,0:T(8,128)(2,1)S(1)}, u32[]{:S(2)}, u32[]{:S(2)}) collective-permute-start(bf16[32,2048]{1,0:T(8,128)(2,1)S(1)} %constant_dynamic-update-slice_fusion.refs_0_), channel_id=1, source_target_pairs={{0,4},{4,0},{8,12},{12,8},{16,20},{20,16},{24,28},{28,24},{1,5},{5... | collective-permute-start | bytes 393224 | tf_op jit(solution)/shard_map/ppermute | solution.py:145
  44.9 5.0 %collective-permute-start.15 = (bf16[32,2048]{1,0:T(8,128)(2,1)S(1)}, bf16[32,2048]{1,0:T(8,128)(2,1)S(1)}, u32[]{:S(2)}, u32[]{:S(2)}) collective-permute-start(bf16[32,2048]{1,0:T(8,128)(2,1)S(1)} %collective-permute-done.13.refs_9_), channel_id=1, source_target_pairs={{0,8},{4,12},{8,0},{12,4},{16,24},{20,28},{24,16},{28,20},{1,9},{5... | collective-permute-start | bytes 393224 | tf_op jit(solution)/shard_map/ppermute | solution.py:145
  44.9 5.0 %collective-permute-start.17 = (bf16[32,2048]{1,0:T(8,128)(2,1)S(1)}, bf16[32,2048]{1,0:T(8,128)(2,1)S(1)}, u32[]{:S(2)}, u32[]{:S(2)}) collective-permute-start(bf16[32,2048]{1,0:T(8,128)(2,1)S(1)} %collective-permute-done.13.refs_9_), channel_id=1, source_target_pairs={{0,4},{4,0},{8,12},{12,8},{16,20},{20,16},{24,28},{28,24},{1,5},{5... | collective-permute-start | bytes 393224 | tf_op jit(solution)/shard_map/ppermute | solution.py:145
  47.6 5.0 %collective-permute-start.6 = (bf16[32,2048]{1,0:T(8,128)(2,1)S(1)}, bf16[32,2048]{1,0:T(8,128)(2,1)S(1)}, u32[]{:S(2)}, u32[]{:S(2)}) collective-permute-start(bf16[32,2048]{1,0:T(8,128)(2,1)S(1)} %collective-permute-done.4.refs_1_), channel_id=1, source_target_pairs={{0,16},{4,20},{8,24},{12,28},{16,0},{20,4},{24,8},{28,12},{1,17},{... | collective-permute-start | bytes 393224 | tf_op jit(solution)/shard_map/ppermute | solution.py:145
  47.7 5.7 %collective-permute-start.8 = (bf16[32,2048]{1,0:T(8,128)(2,1)S(1)}, bf16[32,2048]{1,0:T(8,128)(2,1)S(1)}, u32[]{:S(2)}, u32[]{:S(2)}) collective-permute-start(bf16[32,2048]{1,0:T(8,128)(2,1)S(1)} %collective-permute-done.4.refs_1_), channel_id=1, source_target_pairs={{0,4},{4,0},{8,12},{12,8},{16,20},{20,16},{24,28},{28,24},{1,5},{5... | collective-permute-start | bytes 393224 | tf_op jit(solution)/shard_map/ppermute | solution.py:145
  47.8 5.0 %collective-permute-start.18 = (bf16[32,2048]{1,0:T(8,128)(2,1)S(1)}, bf16[32,2048]{1,0:T(8,128)(2,1)S(1)}, u32[]{:S(2)}, u32[]{:S(2)}) collective-permute-start(bf16[32,2048]{1,0:T(8,128)(2,1)S(1)} %collective-permute-done.14.refs_10_), channel_id=1, source_target_pairs={{0,4},{4,0},{8,12},{12,8},{16,20},{20,16},{24,28},{28,24},{1,5},{5... | collective-permute-start | bytes 393224 | tf_op jit(solution)/shard_map/ppermute | solution.py:145
  49.8 4.2 %collective-permute-start.9 = (bf16[32,2048]{1,0:T(8,128)(2,1)S(1)}, bf16[32,2048]{1,0:T(8,128)(2,1)S(1)}, u32[]{:S(2)}, u32[]{:S(2)}) collective-permute-start(bf16[32,2048]{1,0:T(8,128)(2,1)S(1)} %collective-permute-done.5.refs_2_), channel_id=1, source_target_pairs={{0,4},{4,0},{8,12},{12,8},{16,20},{20,16},{24,28},{28,24},{1,5},{5... | collective-permute-start | bytes 393224 | tf_op jit(solution)/shard_map/ppermute | solution.py:145
  49.8 4.9 %collective-permute-start.19 = (bf16[32,2048]{1,0:T(8,128)(2,1)S(1)}, bf16[32,2048]{1,0:T(8,128)(2,1)S(1)}, u32[]{:S(2)}, u32[]{:S(2)}) collective-permute-start(bf16[32,2048]{1,0:T(8,128)(2,1)S(1)} %collective-permute-done.15.refs_11_), channel_id=1, source_target_pairs={{0,4},{4,0},{8,12},{12,8},{16,20},{20,16},{24,28},{28,24},{1,5},{5... | collective-permute-start | bytes 393224 | tf_op jit(solution)/shard_map/ppermute | solution.py:145
  52.5 2.8 %collective-permute-start.10 = (bf16[32,2048]{1,0:T(8,128)(2,1)S(1)}, bf16[32,2048]{1,0:T(8,128)(2,1)S(1)}, u32[]{:S(2)}, u32[]{:S(2)}) collective-permute-start(bf16[32,2048]{1,0:T(8,128)(2,1)S(1)} %collective-permute-done.6.refs_3_), channel_id=1, source_target_pairs={{0,4},{4,0},{8,12},{12,8},{16,20},{20,16},{24,28},{28,24},{1,5},{5... | collective-permute-start | bytes 393224 | tf_op jit(solution)/shard_map/ppermute | solution.py:145
  52.7 0.6 copy-start.2
  53.4 0.7 copy-start
  54.1 0.7 copy-start.4
  54.7 0.7 copy-start.6
  55.4 0.7 copy-start.8
  56.0 0.9 copy-start.1
  56.9 0.9 copy-start.3
  57.8 0.9 copy-start.5
  58.7 0.9 copy-start.7
  59.6 0.9 copy-start.9
  69.3 25.1 %collective-permute-start.20 = (bf16[128,1792]{1,0:T(8,128)(2,1)S(1)}, bf16[128,1792]{1,0:T(8,128)(2,1)S(1)}, u32[]{:S(2)}, u32[]{:S(2)}) collective-permute-start(bf16[128,1792]{1,0:T(8,128)(2,1)S(1)} %get-tuple-element.12), channel_id=1, source_target_pairs={{0,1},{4,5},{8,9},{12,13},{16,17},{20,21},{24,25},{28,29}} | collective-permute-start | bytes 1376264 | tf_op jit(solution)/shard_map/ppermute | solution.py:160
  70.6 39.1 %collective-permute-start.23 = (bf16[128,1792]{1,0:T(8,128)(2,1)S(1)}, bf16[128,1792]{1,0:T(8,128)(2,1)S(1)}, u32[]{:S(2)}, u32[]{:S(2)}) collective-permute-start(bf16[128,1792]{1,0:T(8,128)(2,1)S(1)} %get-tuple-element.13), channel_id=1, source_target_pairs={{3,2},{7,6},{11,10},{15,14},{19,18},{23,22},{27,26},{31,30}} | collective-permute-start | bytes 1376264 | tf_op jit(solution)/shard_map/ppermute | solution.py:160
  79.3 28.4 %collective-permute-start.26 = (bf16[128,1792]{1,0:T(8,128)(2,1)S(1)}, bf16[128,1792]{1,0:T(8,128)(2,1)S(1)}, u32[]{:S(2)}, u32[]{:S(2)}) collective-permute-start(bf16[128,1792]{1,0:T(8,128)(2,1)S(1)} %get-tuple-element.16), channel_id=1, source_target_pairs={{0,1},{4,5},{8,9},{12,13},{16,17},{20,21},{24,25},{28,29}} | collective-permute-start | bytes 1376264 | tf_op jit(solution)/shard_map/ppermute | solution.py:160
  80.6 43.0 %collective-permute-start.29 = (bf16[128,1792]{1,0:T(8,128)(2,1)S(1)}, bf16[128,1792]{1,0:T(8,128)(2,1)S(1)}, u32[]{:S(2)}, u32[]{:S(2)}) collective-permute-start(bf16[128,1792]{1,0:T(8,128)(2,1)S(1)} %get-tuple-element.17), channel_id=1, source_target_pairs={{3,2},{7,6},{11,10},{15,14},{19,18},{23,22},{27,26},{31,30}} | collective-permute-start | bytes 1376264 | tf_op jit(solution)/shard_map/ppermute | solution.py:160
  94.5 23.0 %collective-permute-start.21 = (bf16[128,1792]{1,0:T(8,128)(2,1)S(1)}, bf16[128,1792]{1,0:T(8,128)(2,1)S(1)}, u32[]{:S(2)}, u32[]{:S(2)}) collective-permute-start(bf16[128,1792]{1,0:T(8,128)(2,1)S(1)} %add_convert_fusion.9), channel_id=1, source_target_pairs={{0,1},{1,2},{4,5},{5,6},{8,9},{9,10},{12,13},{13,14},{16,17},{17,1... | collective-permute-start | bytes 1376264 | tf_op jit(solution)/shard_map/ppermute | solution.py:160
  107.8 19.5 %collective-permute-start.27 = (bf16[128,1792]{1,0:T(8,128)(2,1)S(1)}, bf16[128,1792]{1,0:T(8,128)(2,1)S(1)}, u32[]{:S(2)}, u32[]{:S(2)}) collective-permute-start(bf16[128,1792]{1,0:T(8,128)(2,1)S(1)} %add_convert_fusion.4), channel_id=1, source_target_pairs={{0,1},{1,2},{4,5},{5,6},{8,9},{9,10},{12,13},{13,14},{16,17},{17,1... | collective-permute-start | bytes 1376264 | tf_op jit(solution)/shard_map/ppermute | solution.py:160
  117.8 15.7 %collective-permute-start.24 = (bf16[128,1792]{1,0:T(8,128)(2,1)S(1)}, bf16[128,1792]{1,0:T(8,128)(2,1)S(1)}, u32[]{:S(2)}, u32[]{:S(2)}) collective-permute-start(bf16[128,1792]{1,0:T(8,128)(2,1)S(1)} %get-tuple-element.11), channel_id=1, source_target_pairs={{2,1},{3,2},{6,5},{7,6},{10,9},{11,10},{14,13},{15,14},{18,17},{19... | collective-permute-start | bytes 1376264 | tf_op jit(solution)/shard_map/ppermute | solution.py:160
  119.1 25.9 %collective-permute-start.22 = (bf16[128,1792]{1,0:T(8,128)(2,1)S(1)}, bf16[128,1792]{1,0:T(8,128)(2,1)S(1)}, u32[]{:S(2)}, u32[]{:S(2)}) collective-permute-start(bf16[128,1792]{1,0:T(8,128)(2,1)S(1)} %get-tuple-element.10), channel_id=1, source_target_pairs={{0,1},{1,2},{2,3},{4,5},{5,6},{6,7},{8,9},{9,10},{10,11},{12,13},{... | collective-permute-start | bytes 1376264 | tf_op jit(solution)/shard_map/ppermute | solution.py:160
  127.6 15.3 %collective-permute-start.30 = (bf16[128,1792]{1,0:T(8,128)(2,1)S(1)}, bf16[128,1792]{1,0:T(8,128)(2,1)S(1)}, u32[]{:S(2)}, u32[]{:S(2)}) collective-permute-start(bf16[128,1792]{1,0:T(8,128)(2,1)S(1)} %get-tuple-element.15), channel_id=1, source_target_pairs={{2,1},{3,2},{6,5},{7,6},{10,9},{11,10},{14,13},{15,14},{18,17},{19... | collective-permute-start | bytes 1376264 | tf_op jit(solution)/shard_map/ppermute | solution.py:160
  128.9 24.0 %collective-permute-start.28 = (bf16[128,1792]{1,0:T(8,128)(2,1)S(1)}, bf16[128,1792]{1,0:T(8,128)(2,1)S(1)}, u32[]{:S(2)}, u32[]{:S(2)}) collective-permute-start(bf16[128,1792]{1,0:T(8,128)(2,1)S(1)} %get-tuple-element.14), channel_id=1, source_target_pairs={{0,1},{1,2},{2,3},{4,5},{5,6},{6,7},{8,9},{9,10},{10,11},{12,13},{... | collective-permute-start | bytes 1376264 | tf_op jit(solution)/shard_map/ppermute | solution.py:160
  133.6 19.1 %collective-permute-start.25 = (bf16[128,1792]{1,0:T(8,128)(2,1)S(1)}, bf16[128,1792]{1,0:T(8,128)(2,1)S(1)}, u32[]{:S(2)}, u32[]{:S(2)}) collective-permute-start(bf16[128,1792]{1,0:T(8,128)(2,1)S(1)} %add_convert_fusion.6), channel_id=1, source_target_pairs={{1,0},{2,1},{3,2},{5,4},{6,5},{7,6},{9,8},{10,9},{11,10},{13,12},{... | collective-permute-start | bytes 1376264 | tf_op jit(solution)/shard_map/ppermute | solution.py:160
  143.0 18.4 %collective-permute-start.31 = (bf16[128,1792]{1,0:T(8,128)(2,1)S(1)}, bf16[128,1792]{1,0:T(8,128)(2,1)S(1)}, u32[]{:S(2)}, u32[]{:S(2)}) collective-permute-start(bf16[128,1792]{1,0:T(8,128)(2,1)S(1)} %add_convert_fusion.1), channel_id=1, source_target_pairs={{1,0},{2,1},{3,2},{5,4},{6,5},{7,6},{9,8},{10,9},{11,10},{13,12},{... | collective-permute-start | bytes 1376264 | tf_op jit(solution)/shard_map/ppermute | solution.py:160
Sparse Core Ops, SparseCore 0:
  13.2 88.5 all-gather.1
